TPU v7x, 256 devices: a whole 4x4x8 slice. The times are simulated.
256 devices in a mesh: pipe: 4 (over z_lo, core), fsdp: 64 (over x, z_hi, y).
Axes of the slice: x: 4, y: 4, z: 8 (z_hi: 4, z_lo: 2; z = z_hi * 2 + z_lo), core: 2. Of those that a mesh axis runs over, the one named last changes fastest.
Arguments:
- tokens: int32 [2, 160], replicated, may hold values from 0 to 511
- embed: bfloat16 [512, 8192], P(None, 'fsdp'), may hold values from -60 to 60
- gain: bfloat16 [4, 8192], P('pipe', 'fsdp'), may hold values from 0.099609375 to 1.8984375
- w_in: bfloat16 [4, 3, 8192, 8192], P('pipe', None, None, 'fsdp'), may hold values from -0.0625 to 0.0625
- short_filter: float32 [4, 3, 7, 8192], P('pipe', None, None, 'fsdp'), may hold values from -2 to 2
- long_filter: float32 [4, 512, 128], P('pipe', 'fsdp'), may hold values from -0.5 to 0.5
- skip_bias: float32 [4, 8192], P('pipe', 'fsdp'), may hold values from -1 to 1
- w_out: bfloat16 [4, 8192, 8192], P('pipe', None, 'fsdp'), may hold values from -0.0625 to 0.0625
Outputs:
- hidden: bfloat16 [2, 160, 8192], P(None, 'pipe', 'fsdp')
All inputs are finite; a program needn't handle non-finite values.
Results may differ from a plain program's by a relative error of at most 0.035.
Values may be sent and summed in bfloat16 or wider, within the bound.
No kernel may reach another device: no remote copies, remote signals or barrier semaphores. Data moves between devices by JAX's collectives and lax.ppermute only.
A program may use at most 64 MiB of HBM per device.

v0:
```python
import jax
import jax.numpy as jnp
from jax import lax
from jax.sharding import PartitionSpec as P

D = 8192
GROUP = 16


def from_behind(block, axis, distance):
    devices = range(lax.axis_size(axis))
    route = [(i - distance, i) for i in devices if i - distance in devices]
    return lax.ppermute(block, axis, route)


def spread(value, axis, root):
    mine = lax.axis_index(axis) == root
    return lax.psum(jnp.where(mine, value, jnp.zeros_like(value)), axis)


def short_mix(projected, filters):
    width = filters.shape[1]
    seq_len = projected.shape[1]
    padded = jnp.pad(projected.astype(jnp.float32), ((0, 0), (width - 1, 0), (0, 0)))
    running = jnp.zeros(projected.shape, jnp.float32)
    for offset in range(width):
        window = padded[:, width - 1 - offset : width - 1 - offset + seq_len, :]
        running = running + filters[:, offset][:, None, :] * window
    return running


def long_mix(signal, kernels, group_size):
    seq_len = signal.shape[0]
    span = kernels.shape[1]
    count_filters = kernels.shape[0]
    positions = jnp.arange(seq_len, dtype=jnp.int32)
    lag_table = positions[:, None] - positions[None, :]
    inside = (lag_table >= 0) & (lag_table < span)
    lag_index = jnp.clip(lag_table, 0, span - 1)
    toeplitz = jnp.where(inside[None, :, :], kernels[:, lag_index], jnp.float32(0.0))
    grouped = signal.reshape(seq_len, count_filters, group_size)
    mixed = jnp.einsum("fts,sfg->tfg", toeplitz, grouped, precision=lax.Precision.HIGHEST)
    return mixed.reshape(seq_len, count_filters * group_size)


def body(tokens, embed, gain, w_in, short_filter, long_filter, skip_bias, w_out):
    segment_count = lax.axis_size("pipe")
    segment_index = lax.axis_index("pipe")
    batch_count = tokens.shape[0]
    seq_len = tokens.shape[1]
    local_width = embed.shape[1]
    in_weights = w_in[0]
    short_taps = short_filter[0]
    long_taps = long_filter[0]
    skip_row = skip_bias[0]
    out_weight = w_out[0]
    vocab_index = jnp.arange(embed.shape[0], dtype=jnp.int32)

    def layer_step(activation):
        widened = activation.astype(jnp.float32)
        squares = lax.psum(jnp.sum(widened * widened, axis=1), "fsdp")
        inverse_rms = lax.rsqrt(squares / D + 1e-06)[:, None]
        normalized = (widened * inverse_rms * gain.astype(jnp.float32)).astype(jnp.bfloat16)
        weight_rows = in_weights
        projected = jnp.einsum(
            "sk,jkc->jsc",
            lax.all_gather(normalized, "fsdp", axis=1, tiled=True),
            weight_rows,
            preferred_element_type=jnp.float32,
        )
        mixed = short_mix(projected.astype(jnp.bfloat16), short_taps)
        product = mixed[1] * mixed[2]
        carried = long_mix(product, long_taps, GROUP) + skip_row[None, :] * product
        gated = (mixed[0] * carried).astype(jnp.bfloat16)
        weight_rows = out_weight
        projected_out = jnp.dot(
            lax.all_gather(gated, "fsdp", axis=1, tiled=True),
            weight_rows,
            preferred_element_type=jnp.float32,
        )
        return (widened + projected_out).astype(jnp.bfloat16)

    def tick_body(tick_index, carry_state):
        previous, collected = carry_state
        incoming = from_behind(previous, "pipe", 1)
        micro_index = tick_index - segment_index
        chosen = jnp.clip(micro_index, 0, batch_count - 1)
        token_ids = lax.dynamic_index_in_dim(tokens, chosen, 0, keepdims=False)
        one_hot = (token_ids[:, None] == vocab_index[None, :]).astype(jnp.bfloat16)
        embedded = jnp.dot(one_hot, embed, preferred_element_type=jnp.float32).astype(jnp.bfloat16)
        activation = jnp.where(segment_index == 0, embedded, incoming)
        layer_out = layer_step(activation)
        store_flag = (
            (micro_index >= 0) & (micro_index < batch_count) & (segment_index == segment_count - 1)
        )
        updated = lax.dynamic_update_index_in_dim(collected, layer_out, chosen, 0)
        collected = jnp.where(store_flag, updated, collected)
        return (layer_out, collected)

    start_state = (
        jnp.zeros((seq_len, local_width), jnp.bfloat16),
        jnp.zeros((batch_count, seq_len, local_width), jnp.bfloat16),
    )
    final_state = lax.fori_loop(0, batch_count + segment_count - 1, tick_body, start_state)
    finished = spread(final_state[1], "pipe", segment_count - 1)
    row_share = seq_len // segment_count
    return lax.dynamic_slice_in_dim(finished, segment_index * row_share, row_share, 1)


def solution(mesh):
    return jax.shard_map(
        body,
        mesh=mesh,
        in_specs=(
            P(),
            P(None, "fsdp"),
            P("pipe", "fsdp"),
            P("pipe", None, None, "fsdp"),
            P("pipe", None, None, "fsdp"),
            P("pipe", "fsdp", None),
            P("pipe", "fsdp"),
            P("pipe", None, "fsdp"),
        ),
        out_specs=P(None, "pipe", "fsdp"),
        check_vma=False,
    )
```

profile of v0, /device:TPU:1, one launch (start us, length us, event | category | flops | bytes accessed | tf_op | source)
XLA Modules:
  0.0 2043.1 jit_solution(8263287136697875596)
XLA Ops:
  10.1 1982.0 %while.18 = (s32[]{:T(128)}, bf16[160,128]{1,0:T(8,128)(2,1)}, bf16[2,160,128]{2,1,0:T(8,128)(2,1)}, pred[]{:T(512)}, s32[]{:T(128)}, /*index=5*/s32[2,160]{1,0:...) while((s32[]{:T(128)}, bf16[160,128]{1,0:T(8,128)(2,1)}, ...), condition=%wide.region_3.4_spmd.clone, body=%wide.region_0.3_spmd.clone.sunk | while | flops 1404303872 | bytes 46493152 | solution.py:104
  10.1 4.9 collective-permute-start
  17.7 168.4 %psum.24 = f32[160]{0:T(256)S(1)} all-reduce(f32[160]{0:T(256)S(1)} %get-tuple-element.508), channel_id=1, replica_groups=mesh['pipe'=4,'fsdp'=64] {'fsdp'}, use_global_device_ids=true, to_apply=%region_2.2 | all-reduce | flops 160 | bytes 1280 | tf_op jit(solution)/shard_map/while/body/eval_jaxpr/psum | solution.py:61
  187.1 85.3 %gather_fusion = f32[25600,8]{1,0:T(8,128)} fusion(f32[8,128]{0,1:T(8,128)S(1)} %get-tuple-element.562, s32[25600]{0:T(1024)S(1)} %broadcast_clamp_fusion.2), kind=kCustom, calls=%fused_computation.clone.clone.1 | custom fusion | bytes 1740800 | tf_op jit(solution)/shard_map/while/body/eval_jaxpr/gather | solution.py:40
  272.4 8.8 copy.25
  283.2 13.5 all-gather.3.cloned.1.call-done
  296.7 5.1 fusion.56
  303.4 1.6 copy.24
  305.1 2.8 fusion.58
  310.4 96.4 %all-gather.5.cloned.1.call-done = bf16[160,8192]{1,0:T(8,128)(2,1)} async-done(((bf16[160,128]{1,0:T(8,128)(2,1)}), bf16[160,8192]{1,0:T(8,128)(2,1)}) %all-gather.5.cloned.1.call-update) | async-done | bytes 2621456 | tf_op jit(solution)/shard_map/while/body/eval_jaxpr/all_gather | solution.py:77
  406.9 3.2 fusion.60
  410.9 1.9 collective-permute-start
  415.4 166.0 %psum.24 = f32[160]{0:T(256)S(1)} all-reduce(f32[160]{0:T(256)S(1)} %get-tuple-element.508), channel_id=1, replica_groups=mesh['pipe'=4,'fsdp'=64] {'fsdp'}, use_global_device_ids=true, to_apply=%region_2.2 | all-reduce | flops 160 | bytes 1280 | tf_op jit(solution)/shard_map/while/body/eval_jaxpr/psum | solution.py:61
  582.4 85.3 %gather_fusion = f32[25600,8]{1,0:T(8,128)} fusion(f32[8,128]{0,1:T(8,128)S(1)} %get-tuple-element.562, s32[25600]{0:T(1024)S(1)} %broadcast_clamp_fusion.2), kind=kCustom, calls=%fused_computation.clone.clone.1 | custom fusion | bytes 1740800 | tf_op jit(solution)/shard_map/while/body/eval_jaxpr/gather | solution.py:40
  667.6 8.8 copy.25
  678.5 13.8 all-gather.3.cloned.1.call-done
  692.3 5.1 fusion.56
  700.7 2.8 fusion.58
  706.1 96.3 %all-gather.5.cloned.1.call-done = bf16[160,8192]{1,0:T(8,128)(2,1)} async-done(((bf16[160,128]{1,0:T(8,128)(2,1)}), bf16[160,8192]{1,0:T(8,128)(2,1)}) %all-gather.5.cloned.1.call-update) | async-done | bytes 2621456 | tf_op jit(solution)/shard_map/while/body/eval_jaxpr/all_gather | solution.py:77
  802.4 3.2 fusion.60
  806.4 1.9 collective-permute-start
  810.9 166.0 %psum.24 = f32[160]{0:T(256)S(1)} all-reduce(f32[160]{0:T(256)S(1)} %get-tuple-element.508), channel_id=1, replica_groups=mesh['pipe'=4,'fsdp'=64] {'fsdp'}, use_global_device_ids=true, to_apply=%region_2.2 | all-reduce | flops 160 | bytes 1280 | tf_op jit(solution)/shard_map/while/body/eval_jaxpr/psum | solution.py:61
  977.9 85.3 %gather_fusion = f32[25600,8]{1,0:T(8,128)} fusion(f32[8,128]{0,1:T(8,128)S(1)} %get-tuple-element.562, s32[25600]{0:T(1024)S(1)} %broadcast_clamp_fusion.2), kind=kCustom, calls=%fused_computation.clone.clone.1 | custom fusion | bytes 1740800 | tf_op jit(solution)/shard_map/while/body/eval_jaxpr/gather | solution.py:40
  1063.1 8.8 copy.25
  1074.0 13.8 all-gather.3.cloned.1.call-done
  1087.8 5.1 fusion.56
  1096.2 2.8 fusion.58
  1101.6 96.3 %all-gather.5.cloned.1.call-done = bf16[160,8192]{1,0:T(8,128)(2,1)} async-done(((bf16[160,128]{1,0:T(8,128)(2,1)}), bf16[160,8192]{1,0:T(8,128)(2,1)}) %all-gather.5.cloned.1.call-update) | async-done | bytes 2621456 | tf_op jit(solution)/shard_map/while/body/eval_jaxpr/all_gather | solution.py:77
  1197.9 3.2 fusion.60
  1201.9 1.9 collective-permute-start
  1206.4 166.0 %psum.24 = f32[160]{0:T(256)S(1)} all-reduce(f32[160]{0:T(256)S(1)} %get-tuple-element.508), channel_id=1, replica_groups=mesh['pipe'=4,'fsdp'=64] {'fsdp'}, use_global_device_ids=true, to_apply=%region_2.2 | all-reduce | flops 160 | bytes 1280 | tf_op jit(solution)/shard_map/while/body/eval_jaxpr/psum | solution.py:61
  1373.4 85.3 %gather_fusion = f32[25600,8]{1,0:T(8,128)} fusion(f32[8,128]{0,1:T(8,128)S(1)} %get-tuple-element.562, s32[25600]{0:T(1024)S(1)} %broadcast_clamp_fusion.2), kind=kCustom, calls=%fused_computation.clone.clone.1 | custom fusion | bytes 1740800 | tf_op jit(solution)/shard_map/while/body/eval_jaxpr/gather | solution.py:40
  1458.6 8.8 copy.25
  1469.5 13.8 all-gather.3.cloned.1.call-done
  1483.3 5.1 fusion.56
  1491.7 2.8 fusion.58
  1497.1 96.3 %all-gather.5.cloned.1.call-done = bf16[160,8192]{1,0:T(8,128)(2,1)} async-done(((bf16[160,128]{1,0:T(8,128)(2,1)}), bf16[160,8192]{1,0:T(8,128)(2,1)}) %all-gather.5.cloned.1.call-update) | async-done | bytes 2621456 | tf_op jit(solution)/shard_map/while/body/eval_jaxpr/all_gather | solution.py:77
  1593.4 3.2 fusion.60
  1597.4 1.9 collective-permute-start
  1601.9 166.0 %psum.24 = f32[160]{0:T(256)S(1)} all-reduce(f32[160]{0:T(256)S(1)} %get-tuple-element.508), channel_id=1, replica_groups=mesh['pipe'=4,'fsdp'=64] {'fsdp'}, use_global_device_ids=true, to_apply=%region_2.2 | all-reduce | flops 160 | bytes 1280 | tf_op jit(solution)/shard_map/while/body/eval_jaxpr/psum | solution.py:61
  1768.9 85.3 %gather_fusion = f32[25600,8]{1,0:T(8,128)} fusion(f32[8,128]{0,1:T(8,128)S(1)} %get-tuple-element.562, s32[25600]{0:T(1024)S(1)} %broadcast_clamp_fusion.2), kind=kCustom, calls=%fused_computation.clone.clone.1 | custom fusion | bytes 1740800 | tf_op jit(solution)/shard_map/while/body/eval_jaxpr/gather | solution.py:40
  1854.1 8.8 copy.25
  1865.0 13.8 all-gather.3.cloned.1.call-done
  1878.8 5.1 fusion.56
  1887.2 2.8 fusion.58
  1892.6 96.3 %all-gather.5.cloned.1.call-done = bf16[160,8192]{1,0:T(8,128)(2,1)} async-done(((bf16[160,128]{1,0:T(8,128)(2,1)}), bf16[160,8192]{1,0:T(8,128)(2,1)}) %all-gather.5.cloned.1.call-update) | async-done | bytes 2621456 | tf_op jit(solution)/shard_map/while/body/eval_jaxpr/all_gather | solution.py:77
  1988.9 3.2 fusion.60
  1992.7 41.6 %all-reduce.3.cloned.1.call-done = bf16[2,160,128]{2,1,0:T(8,128)(2,1)} async-done(((bf16[2,160,128]{2,1,0:T(8,128)(2,1)}), bf16[2,160,128]{2,1,0:T(8,128)(2,1)}) %all-reduce.3.cloned.1.call-update) | async-done | bytes 81936 | tf_op jit(solution)/shard_map/psum | solution.py:18
  (202 shorter events, 63.4 us)
Async XLA Ops:
  10.1 286.6 %all-gather.3.cloned.1.call-start = ((), (), s32[]{:S(2)}) async-start(), calls=%async_computation.1 | async-start | bytes 2662400 | tf_op jit(solution)/shard_map/while/body/eval_jaxpr/all_gather | solution.py:67
  10.1 6.3 collective-permute-start
  186.8 220.0 %all-gather.5.cloned.1.call-start = ((), (), s32[]{:S(2)}) async-start(), calls=%async_computation.2 | async-start | bytes 2662400 | tf_op jit(solution)/shard_map/while/body/eval_jaxpr/all_gather | solution.py:77
  296.7 5.2 copy-start.4
  296.7 5.2 copy-start.5
  296.7 5.2 copy-start.6
  296.7 5.2 copy-start.7
  296.7 5.2 copy-start.8
  301.8 105.1 %copy-start = (bf16[8192,128]{1,0:T(8,128)(2,1)S(1)}, bf16[8192,128]{1,0:T(8,128)(2,1)}, u32[]{:S(2)}) copy-start(bf16[8192,128]{1,0:T(8,128)(2,1)} %get-tuple-element.564) | copy-start | bytes 6291460 | tf_op jit(solution)/shard_map/while
  410.1 282.2 %all-gather.3.cloned.1.call-start = ((), (), s32[]{:S(2)}) async-start(), calls=%async_computation.1 | async-start | bytes 2662400 | tf_op jit(solution)/shard_map/while/body/eval_jaxpr/all_gather | solution.py:67
  410.9 3.3 collective-permute-start
  582.1 220.2 %all-gather.5.cloned.1.call-start = ((), (), s32[]{:S(2)}) async-start(), calls=%async_computation.2 | async-start | bytes 2662400 | tf_op jit(solution)/shard_map/while/body/eval_jaxpr/all_gather | solution.py:77
  692.3 5.2 copy-start.3
  692.3 5.2 copy-start.4
  692.3 5.2 copy-start.5
  692.3 5.2 copy-start.6
  692.3 5.2 copy-start.7
  692.3 5.2 copy-start.8
  697.4 104.9 %copy-start = (bf16[8192,128]{1,0:T(8,128)(2,1)S(1)}, bf16[8192,128]{1,0:T(8,128)(2,1)}, u32[]{:S(2)}) copy-start(bf16[8192,128]{1,0:T(8,128)(2,1)} %get-tuple-element.564) | copy-start | bytes 6291460 | tf_op jit(solution)/shard_map/while
  805.6 282.2 %all-gather.3.cloned.1.call-start = ((), (), s32[]{:S(2)}) async-start(), calls=%async_computation.1 | async-start | bytes 2662400 | tf_op jit(solution)/shard_map/while/body/eval_jaxpr/all_gather | solution.py:67
  806.4 3.3 collective-permute-start
  977.6 220.2 %all-gather.5.cloned.1.call-start = ((), (), s32[]{:S(2)}) async-start(), calls=%async_computation.2 | async-start | bytes 2662400 | tf_op jit(solution)/shard_map/while/body/eval_jaxpr/all_gather | solution.py:77
  1087.8 5.2 copy-start.3
  1087.8 5.2 copy-start.4
  1087.8 5.2 copy-start.5
  1087.8 5.2 copy-start.6
  1087.8 5.2 copy-start.7
  1087.8 5.2 copy-start.8
  1093.0 104.9 %copy-start = (bf16[8192,128]{1,0:T(8,128)(2,1)S(1)}, bf16[8192,128]{1,0:T(8,128)(2,1)}, u32[]{:S(2)}) copy-start(bf16[8192,128]{1,0:T(8,128)(2,1)} %get-tuple-element.564) | copy-start | bytes 6291460 | tf_op jit(solution)/shard_map/while
  1201.1 282.2 %all-gather.3.cloned.1.call-start = ((), (), s32[]{:S(2)}) async-start(), calls=%async_computation.1 | async-start | bytes 2662400 | tf_op jit(solution)/shard_map/while/body/eval_jaxpr/all_gather | solution.py:67
  1201.9 3.3 collective-permute-start
  1373.1 220.2 %all-gather.5.cloned.1.call-start = ((), (), s32[]{:S(2)}) async-start(), calls=%async_computation.2 | async-start | bytes 2662400 | tf_op jit(solution)/shard_map/while/body/eval_jaxpr/all_gather | solution.py:77
  1483.3 5.2 copy-start.4
  1483.3 5.2 copy-start.5
  1483.3 5.2 copy-start.6
  1483.3 5.2 copy-start.7
  1483.3 5.2 copy-start.8
  1488.4 104.9 %copy-start = (bf16[8192,128]{1,0:T(8,128)(2,1)S(1)}, bf16[8192,128]{1,0:T(8,128)(2,1)}, u32[]{:S(2)}) copy-start(bf16[8192,128]{1,0:T(8,128)(2,1)} %get-tuple-element.564) | copy-start | bytes 6291460 | tf_op jit(solution)/shard_map/while
  1596.6 282.2 %all-gather.3.cloned.1.call-start = ((), (), s32[]{:S(2)}) async-start(), calls=%async_computation.1 | async-start | bytes 2662400 | tf_op jit(solution)/shard_map/while/body/eval_jaxpr/all_gather | solution.py:67
  1597.4 3.3 collective-permute-start
  1768.6 220.2 %all-gather.5.cloned.1.call-start = ((), (), s32[]{:S(2)}) async-start(), calls=%async_computation.2 | async-start | bytes 2662400 | tf_op jit(solution)/shard_map/while/body/eval_jaxpr/all_gather | solution.py:77
  1878.8 5.2 copy-start.4
  1878.8 5.2 copy-start.5
  1878.8 5.2 copy-start.6
  1878.8 5.2 copy-start.7
  1878.8 5.2 copy-start.8
  1883.9 104.9 %copy-start = (bf16[8192,128]{1,0:T(8,128)(2,1)S(1)}, bf16[8192,128]{1,0:T(8,128)(2,1)}, u32[]{:S(2)}) copy-start(bf16[8192,128]{1,0:T(8,128)(2,1)} %get-tuple-element.564) | copy-start | bytes 6291460 | tf_op jit(solution)/shard_map/while
  1992.1 42.3 %all-reduce.3.cloned.1.call-start = ((), (), s32[]{:S(2)}) async-start(), calls=%async_computation | async-start | bytes 163840 | tf_op jit(solution)/shard_map/psum | solution.py:18
  (13 other events, 44.7 us)
Sparse Core Ops, SparseCore 0:
  187.0 109.6 all-gather.2
  310.6 96.2 all-gather.4
  582.2 110.0 all-gather.2
  706.2 96.1 all-gather.4
  977.7 110.0 all-gather.2
  1101.7 96.1 all-gather.4
  1373.2 110.0 all-gather.2
  1497.2 96.1 all-gather.4
  1768.7 110.0 all-gather.2
  1892.7 96.1 all-gather.4
Sparse Core Ops, SparseCore 1:
  1995.2 39.2 all-reduce.2
where the time goes:
time: 2050 us; the launch traced here: 2040 us
  blocking collectives  832 us (41%)
  waiting for transfers between devices  592 us (29%)
  local copies, waits for them, and re-layouts  502 us (24%)
  matrix products  61.6 us (3%)
  other arithmetic  26.4 us (1%)
    psum x5, blocking collectives, layer_step(): squares = lax.psum(jnp.sum(widened * widened, axis=1), 'fsdp')  832 us
    all_gather x5, waiting for transfers between devices, layer_step(): lax.all_gather(gated, 'fsdp', axis=1, tiled=True)  482 us
    gather x10, local copies, waits for them, and re-layouts, long_mix(): kernels[:, lag_index]  470 us
    all_gather x5, waiting for transfers between devices, layer_step(): lax.all_gather(normalized, 'fsdp', axis=1, tiled=True)  68.8 us
    psum x1, waiting for transfers between devices, spread(): return lax.psum(jnp.where(mine, value, jnp.zeros_like(value)), axis)  41.6 us
  transfers between devices with their start and end apart: 16, of which 11 were waited for; matrix products, arithmetic and copies ran while one was open for 24% of the time, Pallas kernels for 0%

commit v1 on v0

--- a/solution.py
+++ b/solution.py
@@ -62,9 +62,18 @@
         inverse_rms = lax.rsqrt(squares / D + 1e-06)[:, None]
         normalized = (widened * inverse_rms * gain.astype(jnp.float32)).astype(jnp.bfloat16)
         weight_rows = in_weights
+        start_the_rates = lambda s0, axis_name: jnp.concatenate(
+            lax.all_to_all(
+                jnp.stack([s0 for _ in range(lax.axis_size(axis_name))], axis=0),
+                axis_name=axis_name,
+                split_axis=0,
+                concat_axis=0,
+            ),
+            axis=1,
+        )
         projected = jnp.einsum(
             "sk,jkc->jsc",
-            lax.all_gather(normalized, "fsdp", axis=1, tiled=True),
+            start_the_rates(normalized, "fsdp"),
             weight_rows,
             preferred_element_type=jnp.float32,
         )

time: 2050 us -> 2210 us (1.078)
  waiting for transfers between devices: 592 us -> 683 us
  local copies, waits for them, and re-layouts: 502 us -> 553 us
  starting transfers between devices: 12.8 us -> 36.4 us
    all_gather x5, waiting for transfers between devices: 482 us -> 641 us  [layer_step(): lax.all_gather(gated, 'fsdp', axis=1, tiled=True)]
    all_gather x5 -> x0, waiting for transfers between devices: 68.8 us -> none  [layer_step(): lax.all_gather(normalized, 'fsdp', axis=1, tiled=True)]
    reshape x0 -> x10, local copies, waits for them, and re-layouts: none -> 38.5 us  [layer_step(): jnp.concatenate(lax.all_to_all(jnp.stack([s0 for _ in range(lax.axis_size...]
    all_to_all x0 -> x5, starting transfers between devices: none -> 23.6 us  [layer_step(): lax.all_to_all(jnp.stack([s0 for _ in range(lax.axis_size(axis_name))], a...]
  transfers between devices with their start and end apart: 16 -> 16, of which waited for: 11 -> 6; matrix products, arithmetic and copies ran while one was open for 24% -> 22% of each run, Pallas kernels for 0% -> 0%
where the time goes in v1:
time: 2210 us; the launch traced here: 2200 us
  blocking collectives  832 us (38%)
  waiting for transfers between devices  683 us (31%)
  local copies, waits for them, and re-layouts  553 us (25%)
  matrix products  61.9 us (3%)
  starting transfers between devices  36.4 us (2%)
    psum x5, blocking collectives, layer_step(): squares = lax.psum(jnp.sum(widened * widened, axis=1), 'fsdp')  832 us
    all_gather x5, waiting for transfers between devices, layer_step(): lax.all_gather(gated, 'fsdp', axis=1, tiled=True)  641 us
    gather x10, local copies, waits for them, and re-layouts, long_mix(): kernels[:, lag_index]  474 us
  transfers between devices with their start and end apart: 16, of which 6 were waited for; matrix products, arithmetic and copies ran while one was open for 22% of the time, Pallas kernels for 0%

profile of v1, /device:TPU:1, one launch (start us, length us, event | category | flops | bytes accessed | tf_op | source)
XLA Modules:
  0.0 2202.6 jit_solution(6869731706732440427)
XLA Ops:
  10.1 2141.7 %while.18 = (s32[]{:T(128)}, bf16[160,128]{1,0:T(8,128)(2,1)S(1)}, bf16[2,160,128]{2,1,0:T(8,128)(2,1)}, pred[]{:T(512)}, s32[]{:T(128)}, /*index=5*/s32[2,160]{...) while((s32[]{:T(128)}, bf16[160,128]{1,0:T(8,128)(2,1)S(1)}, ...), condition=%wide.region_3.4_spmd.clone, body=%wide.region_0.3_spmd.clone.sunk | while | flops 1404303872 | bytes 62795252 | solution.py:113
  10.1 4.9 collective-permute-start
  17.7 168.4 %psum.24 = f32[160]{0:T(256)S(1)} all-reduce(f32[160]{0:T(256)S(1)} %get-tuple-element.508), channel_id=1, replica_groups=mesh['pipe'=4,'fsdp'=64] {'fsdp'}, use_global_device_ids=true, to_apply=%region_2.2 | all-reduce | flops 160 | bytes 1280 | tf_op jit(solution)/shard_map/while/body/eval_jaxpr/psum | solution.py:61
  188.0 4.7 all-to-all-start
  193.0 85.3 %gather_fusion = f32[25600,8]{1,0:T(8,128)} fusion(f32[8,128]{0,1:T(8,128)S(1)} %get-tuple-element.562, s32[25600]{0:T(1024)S(1)} %broadcast_clamp_fusion.2), kind=kCustom, calls=%fused_computation.clone.clone.1 | custom fusion | bytes 1740800 | tf_op jit(solution)/shard_map/while/body/eval_jaxpr/gather | solution.py:40
  278.2 9.5 copy.33
  292.3 5.2 reshape.131
  297.5 5.2 fusion.48
  306.0 2.8 fusion.50
  311.4 123.9 %all-gather.2.cloned.1.call-done = bf16[160,8192]{1,0:T(8,128)(2,1)} async-done(((bf16[160,128]{1,0:T(8,128)(2,1)}), bf16[160,8192]{1,0:T(8,128)(2,1)}) %all-gather.2.cloned.1.call-update) | async-done | bytes 2621456 | tf_op jit(solution)/shard_map/while/body/eval_jaxpr/all_gather | solution.py:86
  435.3 3.2 fusion.52
  443.0 166.0 %psum.24 = f32[160]{0:T(256)S(1)} all-reduce(f32[160]{0:T(256)S(1)} %get-tuple-element.508), channel_id=1, replica_groups=mesh['pipe'=4,'fsdp'=64] {'fsdp'}, use_global_device_ids=true, to_apply=%region_2.2 | all-reduce | flops 160 | bytes 1280 | tf_op jit(solution)/shard_map/while/body/eval_jaxpr/psum | solution.py:61
  610.9 4.7 all-to-all-start
  615.8 85.3 %gather_fusion = f32[25600,8]{1,0:T(8,128)} fusion(f32[8,128]{0,1:T(8,128)S(1)} %get-tuple-element.562, s32[25600]{0:T(1024)S(1)} %broadcast_clamp_fusion.2), kind=kCustom, calls=%fused_computation.clone.clone.1 | custom fusion | bytes 1740800 | tf_op jit(solution)/shard_map/while/body/eval_jaxpr/gather | solution.py:40
  701.1 9.5 copy.33
  715.2 5.2 reshape.131
  720.4 5.2 fusion.48
  728.9 2.8 fusion.50
  734.3 129.4 %all-gather.2.cloned.1.call-done = bf16[160,8192]{1,0:T(8,128)(2,1)} async-done(((bf16[160,128]{1,0:T(8,128)(2,1)}), bf16[160,8192]{1,0:T(8,128)(2,1)}) %all-gather.2.cloned.1.call-update) | async-done | bytes 2621456 | tf_op jit(solution)/shard_map/while/body/eval_jaxpr/all_gather | solution.py:86
  863.7 3.2 fusion.52
  871.5 166.0 %psum.24 = f32[160]{0:T(256)S(1)} all-reduce(f32[160]{0:T(256)S(1)} %get-tuple-element.508), channel_id=1, replica_groups=mesh['pipe'=4,'fsdp'=64] {'fsdp'}, use_global_device_ids=true, to_apply=%region_2.2 | all-reduce | flops 160 | bytes 1280 | tf_op jit(solution)/shard_map/while/body/eval_jaxpr/psum | solution.py:61
  1039.3 4.7 all-to-all-start
  1044.3 85.3 %gather_fusion = f32[25600,8]{1,0:T(8,128)} fusion(f32[8,128]{0,1:T(8,128)S(1)} %get-tuple-element.562, s32[25600]{0:T(1024)S(1)} %broadcast_clamp_fusion.2), kind=kCustom, calls=%fused_computation.clone.clone.1 | custom fusion | bytes 1740800 | tf_op jit(solution)/shard_map/while/body/eval_jaxpr/gather | solution.py:40
  1129.6 9.5 copy.33
  1143.6 5.2 reshape.131
  1148.9 5.2 fusion.48
  1157.3 2.8 fusion.50
  1162.7 129.0 %all-gather.2.cloned.1.call-done = bf16[160,8192]{1,0:T(8,128)(2,1)} async-done(((bf16[160,128]{1,0:T(8,128)(2,1)}), bf16[160,8192]{1,0:T(8,128)(2,1)}) %all-gather.2.cloned.1.call-update) | async-done | bytes 2621456 | tf_op jit(solution)/shard_map/while/body/eval_jaxpr/all_gather | solution.py:86
  1291.7 3.2 fusion.52
  1299.5 166.0 %psum.24 = f32[160]{0:T(256)S(1)} all-reduce(f32[160]{0:T(256)S(1)} %get-tuple-element.508), channel_id=1, replica_groups=mesh['pipe'=4,'fsdp'=64] {'fsdp'}, use_global_device_ids=true, to_apply=%region_2.2 | all-reduce | flops 160 | bytes 1280 | tf_op jit(solution)/shard_map/while/body/eval_jaxpr/psum | solution.py:61
  1467.3 4.7 all-to-all-start
  1472.3 85.3 %gather_fusion = f32[25600,8]{1,0:T(8,128)} fusion(f32[8,128]{0,1:T(8,128)S(1)} %get-tuple-element.562, s32[25600]{0:T(1024)S(1)} %broadcast_clamp_fusion.2), kind=kCustom, calls=%fused_computation.clone.clone.1 | custom fusion | bytes 1740800 | tf_op jit(solution)/shard_map/while/body/eval_jaxpr/gather | solution.py:40
  1557.6 9.5 copy.33
  1571.7 5.2 reshape.131
  1576.9 5.2 fusion.48
  1585.4 2.8 fusion.50
  1590.7 129.4 %all-gather.2.cloned.1.call-done = bf16[160,8192]{1,0:T(8,128)(2,1)} async-done(((bf16[160,128]{1,0:T(8,128)(2,1)}), bf16[160,8192]{1,0:T(8,128)(2,1)}) %all-gather.2.cloned.1.call-update) | async-done | bytes 2621456 | tf_op jit(solution)/shard_map/while/body/eval_jaxpr/all_gather | solution.py:86
  1720.2 3.2 fusion.52
  1727.9 166.0 %psum.24 = f32[160]{0:T(256)S(1)} all-reduce(f32[160]{0:T(256)S(1)} %get-tuple-element.508), channel_id=1, replica_groups=mesh['pipe'=4,'fsdp'=64] {'fsdp'}, use_global_device_ids=true, to_apply=%region_2.2 | all-reduce | flops 160 | bytes 1280 | tf_op jit(solution)/shard_map/while/body/eval_jaxpr/psum | solution.py:61
  1895.8 4.7 all-to-all-start
  1900.8 85.3 %gather_fusion = f32[25600,8]{1,0:T(8,128)} fusion(f32[8,128]{0,1:T(8,128)S(1)} %get-tuple-element.562, s32[25600]{0:T(1024)S(1)} %broadcast_clamp_fusion.2), kind=kCustom, calls=%fused_computation.clone.clone.1 | custom fusion | bytes 1740800 | tf_op jit(solution)/shard_map/while/body/eval_jaxpr/gather | solution.py:40
  1986.0 9.5 copy.33
  2000.1 5.2 reshape.131
  2005.4 5.2 fusion.48
  2013.8 2.8 fusion.50
  2019.2 129.4 %all-gather.2.cloned.1.call-done = bf16[160,8192]{1,0:T(8,128)(2,1)} async-done(((bf16[160,128]{1,0:T(8,128)(2,1)}), bf16[160,8192]{1,0:T(8,128)(2,1)}) %all-gather.2.cloned.1.call-update) | async-done | bytes 2621456 | tf_op jit(solution)/shard_map/while/body/eval_jaxpr/all_gather | solution.py:86
  2148.7 3.2 fusion.52
  2152.5 41.6 %all-reduce.3.cloned.1.call-done = bf16[2,160,128]{2,1,0:T(8,128)(2,1)} async-done(((bf16[2,160,128]{2,1,0:T(8,128)(2,1)}), bf16[2,160,128]{2,1,0:T(8,128)(2,1)}) %all-reduce.3.cloned.1.call-update) | async-done | bytes 81936 | tf_op jit(solution)/shard_map/psum | solution.py:18
  (222 shorter events, 87.9 us)
Async XLA Ops:
  10.1 6.3 collective-permute-start
  188.0 101.8 %all-to-all-start = ((bf16[64,160,128]{2,1,0:T(8,128)(2,1)}), bf16[64,160,128]{2,1,0:T(8,128)(2,1)S(1)}, u32[]{:S(2)}, u32[]{:S(2)}) async-start(bf16[64,160,128]{2,1,0:T(8,128)(2,1)} %stack.8), calls=%async_computation | async-start | bytes 5242880 | tf_op jit(solution)/shard_map/while/body/eval_jaxpr/all_to_all | solution.py:66
  192.7 242.5 %all-gather.2.cloned.1.call-start = ((), (), s32[]{:S(2)}) async-start(), calls=%async_computation.2 | async-start | bytes 2662400 | tf_op jit(solution)/shard_map/while/body/eval_jaxpr/all_gather | solution.py:86
  297.5 5.3 copy-start.5
  297.5 5.3 copy-start.6
  297.5 5.3 copy-start.7
  297.5 5.3 copy-start.8
  297.5 5.3 copy-start.9
  297.5 8.5 copy-start
  302.7 132.5 %copy-start.1 = (bf16[8192,128]{1,0:T(8,128)(2,1)S(1)}, bf16[8192,128]{1,0:T(8,128)(2,1)}, u32[]{:S(2)}) copy-start(bf16[8192,128]{1,0:T(8,128)(2,1)} %get-tuple-element.564) | copy-start | bytes 6291460 | tf_op jit(solution)/shard_map/while
  438.5 3.3 collective-permute-start
  610.9 101.8 %all-to-all-start = ((bf16[64,160,128]{2,1,0:T(8,128)(2,1)}), bf16[64,160,128]{2,1,0:T(8,128)(2,1)S(1)}, u32[]{:S(2)}, u32[]{:S(2)}) async-start(bf16[64,160,128]{2,1,0:T(8,128)(2,1)} %stack.8), calls=%async_computation | async-start | bytes 5242880 | tf_op jit(solution)/shard_map/while/body/eval_jaxpr/all_to_all | solution.py:66
  615.6 248.1 %all-gather.2.cloned.1.call-start = ((), (), s32[]{:S(2)}) async-start(), calls=%async_computation.2 | async-start | bytes 2662400 | tf_op jit(solution)/shard_map/while/body/eval_jaxpr/all_gather | solution.py:86
  720.4 5.3 copy-start.5
  720.4 5.3 copy-start.6
  720.4 5.3 copy-start.7
  720.4 5.3 copy-start.8
  720.4 5.3 copy-start.9
  720.4 8.5 copy-start
  725.6 138.1 %copy-start.1 = (bf16[8192,128]{1,0:T(8,128)(2,1)S(1)}, bf16[8192,128]{1,0:T(8,128)(2,1)}, u32[]{:S(2)}) copy-start(bf16[8192,128]{1,0:T(8,128)(2,1)} %get-tuple-element.564) | copy-start | bytes 6291460 | tf_op jit(solution)/shard_map/while
  866.9 3.3 collective-permute-start
  1039.3 101.8 %all-to-all-start = ((bf16[64,160,128]{2,1,0:T(8,128)(2,1)}), bf16[64,160,128]{2,1,0:T(8,128)(2,1)S(1)}, u32[]{:S(2)}, u32[]{:S(2)}) async-start(bf16[64,160,128]{2,1,0:T(8,128)(2,1)} %stack.8), calls=%async_computation | async-start | bytes 5242880 | tf_op jit(solution)/shard_map/while/body/eval_jaxpr/all_to_all | solution.py:66
  1044.1 247.7 %all-gather.2.cloned.1.call-start = ((), (), s32[]{:S(2)}) async-start(), calls=%async_computation.2 | async-start | bytes 2662400 | tf_op jit(solution)/shard_map/while/body/eval_jaxpr/all_gather | solution.py:86
  1148.8 5.3 copy-start.6
  1148.8 5.3 copy-start.7
  1148.9 5.3 copy-start.8
  1148.9 5.3 copy-start.9
  1148.9 8.5 copy-start
  1154.1 137.6 %copy-start.1 = (bf16[8192,128]{1,0:T(8,128)(2,1)S(1)}, bf16[8192,128]{1,0:T(8,128)(2,1)}, u32[]{:S(2)}) copy-start(bf16[8192,128]{1,0:T(8,128)(2,1)} %get-tuple-element.564) | copy-start | bytes 6291460 | tf_op jit(solution)/shard_map/while
  1294.9 3.3 collective-permute-start
  1467.3 101.8 %all-to-all-start = ((bf16[64,160,128]{2,1,0:T(8,128)(2,1)}), bf16[64,160,128]{2,1,0:T(8,128)(2,1)S(1)}, u32[]{:S(2)}, u32[]{:S(2)}) async-start(bf16[64,160,128]{2,1,0:T(8,128)(2,1)} %stack.8), calls=%async_computation | async-start | bytes 5242880 | tf_op jit(solution)/shard_map/while/body/eval_jaxpr/all_to_all | solution.py:66
  1472.1 248.1 %all-gather.2.cloned.1.call-start = ((), (), s32[]{:S(2)}) async-start(), calls=%async_computation.2 | async-start | bytes 2662400 | tf_op jit(solution)/shard_map/while/body/eval_jaxpr/all_gather | solution.py:86
  1576.8 5.3 copy-start.6
  1576.8 5.3 copy-start.7
  1576.9 5.3 copy-start.8
  1576.9 5.3 copy-start.9
  1576.9 8.5 copy-start
  1582.1 138.1 %copy-start.1 = (bf16[8192,128]{1,0:T(8,128)(2,1)S(1)}, bf16[8192,128]{1,0:T(8,128)(2,1)}, u32[]{:S(2)}) copy-start(bf16[8192,128]{1,0:T(8,128)(2,1)} %get-tuple-element.564) | copy-start | bytes 6291460 | tf_op jit(solution)/shard_map/while
  1723.4 3.3 collective-permute-start
  1895.8 101.8 %all-to-all-start = ((bf16[64,160,128]{2,1,0:T(8,128)(2,1)}), bf16[64,160,128]{2,1,0:T(8,128)(2,1)S(1)}, u32[]{:S(2)}, u32[]{:S(2)}) async-start(bf16[64,160,128]{2,1,0:T(8,128)(2,1)} %stack.8), calls=%async_computation | async-start | bytes 5242880 | tf_op jit(solution)/shard_map/while/body/eval_jaxpr/all_to_all | solution.py:66
  1900.5 248.1 %all-gather.2.cloned.1.call-start = ((), (), s32[]{:S(2)}) async-start(), calls=%async_computation.2 | async-start | bytes 2662400 | tf_op jit(solution)/shard_map/while/body/eval_jaxpr/all_gather | solution.py:86
  2005.3 5.3 copy-start.6
  2005.3 5.3 copy-start.7
  2005.3 5.3 copy-start.8
  2005.3 5.3 copy-start.9
  2005.3 8.5 copy-start
  2010.6 138.1 %copy-start.1 = (bf16[8192,128]{1,0:T(8,128)(2,1)S(1)}, bf16[8192,128]{1,0:T(8,128)(2,1)}, u32[]{:S(2)}) copy-start(bf16[8192,128]{1,0:T(8,128)(2,1)} %get-tuple-element.564) | copy-start | bytes 6291460 | tf_op jit(solution)/shard_map/while
  2151.8 42.3 %all-reduce.3.cloned.1.call-start = ((), (), s32[]{:S(2)}) async-start(), calls=%async_computation.1 | async-start | bytes 163840 | tf_op jit(solution)/shard_map/psum | solution.py:18
  (18 other events, 72.0 us)
Sparse Core Ops, SparseCore 0:
  311.5 123.7 all-gather.1
  734.4 129.2 all-gather.1
  1162.8 128.8 all-gather.1
  1590.8 129.2 all-gather.1
  2019.3 129.2 all-gather.1
Sparse Core Ops, SparseCore 1:
  2154.9 39.2 all-reduce.2
